TPU v7x, 32 devices: a whole 2x2x4 slice. The times are simulated.
32 devices in a mesh: groups: 2 (over x), blk: 16 (over z, y, core).
Axes of the slice: x: 2, y: 2, z: 4, core: 2. Of those that a mesh axis runs over, the one named last changes fastest.
Arguments:
- queries: bfloat16 [24576, 1536], P(('groups', 'blk')), parts along dimension 0, may hold values from -20 to 20
- keys: bfloat16 [24576, 1536], P(('groups', 'blk')), parts along dimension 0, may hold values from -6 to 6
- values: bfloat16 [24576, 1536], P(('groups', 'blk')), parts along dimension 0, may hold values from -6 to 6
- neighbours: int32 [64, 7], P(('groups', 'blk')), parts along dimension 0, may hold values from -1 to 31, as said below
Outputs:
- attended: bfloat16 [24576, 1536], P(('groups', 'blk')), parts along dimension 0
There are 2 independent parts, one for each index of `groups`. A program takes and returns all parts, laid end to end along the dimension named above; each array names one. Nothing has to cross between parts.
Inputs may be any that keep to these rules, and one draw needn't show every extreme that they name: `neighbours`: entry 0 of row t is t itself. Every other non-negative entry names a distinct tile of a frame block at most two blocks away from tile t's block; a slot is -1 only where its drawn tile falls outside the clip.
All inputs are finite; a program needn't handle non-finite values.
Results may differ from a plain program's by a relative error of at most 0.0048.
Values may be sent and summed in bfloat16 or wider, within the bound.
No kernel may reach another device: no remote copies, remote signals or barrier semaphores. Data moves between devices by JAX's collectives and lax.ppermute only.
A program may use at most 128 MiB of HBM per device.

v0:
```python
import jax
import jax.numpy as jnp
from jax import lax
from jax.sharding import PartitionSpec as P

HD = 128


def passed_along(value, axis, steps):
    count = lax.axis_size(axis)
    initial, last = (max(0, -steps), min(count, count - steps))
    return lax.ppermute(value, axis, [(source, source + steps) for source in range(initial, last)])


def on_device(queries, keys, values, neighbours):
    tokens_here = queries.shape[0]
    tiles_here = neighbours.shape[0]
    slots = neighbours.shape[1]
    tile_len = tokens_here // tiles_here
    width = queries.shape[1]
    head_size = HD
    head_count = width // head_size
    scale = head_size ** (-0.5)
    block = lax.axis_index("blk")
    near_low = passed_along((keys, values), "blk", 1)
    near_high = passed_along((keys, values), "blk", -1)
    far_low = passed_along((keys, values), "blk", 2)
    far_high = passed_along((keys, values), "blk", -2)
    window_keys = jnp.concatenate(
        [far_low[0], near_low[0], keys, near_high[0], far_high[0]], axis=0
    )
    window_values = jnp.concatenate(
        [far_low[1], near_low[1], values, near_high[1], far_high[1]], axis=0
    )
    window_keys = window_keys.reshape(5 * tiles_here, tile_len, width)
    window_values = window_values.reshape(5 * tiles_here, tile_len, width)
    base = (block - 2) * tiles_here
    query_tiles = queries.reshape(tiles_here, tile_len, width)

    def one_tile(tile_here):
        named = neighbours[tile_here]
        valid = named >= 0
        local = jnp.where(valid, named - base, 0)
        key_rows = window_keys[local].reshape(slots * tile_len, width)
        value_rows = window_values[local].reshape(slots * tile_len, width)
        query_rows = query_tiles[tile_here]
        key_mask = jnp.repeat(valid, tile_len)[None, :]

        def one_head(head, output):
            start = head * head_size
            query_cols = lax.dynamic_slice_in_dim(query_rows, start, head_size, 1)
            key_cols = lax.dynamic_slice_in_dim(key_rows, start, head_size, 1)
            value_cols = lax.dynamic_slice_in_dim(value_rows, start, head_size, 1)
            scores = (
                lax.dot_general(
                    query_cols,
                    key_cols,
                    (((1,), (1,)), ((), ())),
                    preferred_element_type=jnp.float32,
                )
                * scale
            )
            scores = jnp.where(key_mask, scores, -jnp.inf)
            peak = jnp.max(scores, axis=1, keepdims=True)
            weights = jnp.exp(scores - peak)
            total = jnp.sum(weights, axis=1, keepdims=True)
            rounded = weights.astype(jnp.bfloat16)
            summed = jnp.dot(rounded, value_cols, preferred_element_type=jnp.float32)
            result = (summed / total).astype(jnp.bfloat16)
            return lax.dynamic_update_slice_in_dim(output, result, start, 1)

        empty = jnp.zeros((tile_len, width), jnp.bfloat16)
        return lax.fori_loop(0, head_count, one_head, empty)

    output = lax.map(one_tile, jnp.arange(tiles_here, dtype=jnp.int32))
    return output.reshape(tokens_here, width)


def solution(mesh):
    in_specs = (
        P(("groups", "blk"), None),
        P(("groups", "blk"), None),
        P(("groups", "blk"), None),
        P(("groups", "blk"), None),
    )
    out_specs = P(("groups", "blk"), None)
    return jax.shard_map(
        on_device, mesh=mesh, in_specs=in_specs, out_specs=out_specs, check_vma=False
    )
```

profile of v0, /device:TPU:1, one launch (start us, length us, event | category | flops | bytes accessed | tf_op | source)
XLA Modules:
  0.0 480.4 jit_solution(3247733563765416501)
XLA Ops:
  0.0 5.5 %collective-permute-start.4 = (bf16[768,1536]{1,0:T(8,128)(2,1)}, bf16[768,1536]{1,0:T(8,128)(2,1)}, u32[]{:S(2)}, u32[]{:S(2)}) collective-permute-start(bf16[768,1536]{1,0:T(8,128)(2,1)} %param.10), channel_id=1, source_target_pairs={{0,2},{1,3},{2,4},{3,5},{4,6},{5,7},{6,8},{7,9},{8,10},{9,11},{10,... | collective-permute-start | bytes 7077896 | tf_op jit(solution)/shard_map/ppermute | solution.py:12
  5.5 2.6 collective-permute-start.5
  8.1 4.6 collective-permute-start
  14.6 3.8 collective-permute-start.6
  18.4 61.2 %collective-permute-done.4 = bf16[768,1536]{1,0:T(8,128)(2,1)} collective-permute-done((bf16[768,1536]{1,0:T(8,128)(2,1)}, bf16[768,1536]{1,0:T(8,128)(2,1)}, u32[]{:S(2)}, u32[]{:S(2)}) %collective-permute-start.4) | collective-permute-done | bytes 2359328 | tf_op jit(solution)/shard_map/ppermute | solution.py:12
  80.9 125.1 %collective-permute-done.5 = bf16[768,1536]{1,0:T(8,128)(2,1)} collective-permute-done((bf16[768,1536]{1,0:T(8,128)(2,1)}, bf16[768,1536]{1,0:T(8,128)(2,1)}, u32[]{:S(2)}, u32[]{:S(2)}) %collective-permute-start.5) | collective-permute-done | bytes 2359328 | tf_op jit(solution)/shard_map/ppermute | solution.py:12
  209.7 48.0 %collective-permute-done = bf16[768,1536]{1,0:T(8,128)(2,1)} collective-permute-done((bf16[768,1536]{1,0:T(8,128)(2,1)}, bf16[768,1536]{1,0:T(8,128)(2,1)}, u32[]{:S(2)}, u32[]{:S(2)}) %collective-permute-start) | collective-permute-done | bytes 2359328 | tf_op jit(solution)/shard_map/ppermute | solution.py:12
  262.8 45.5 %collective-permute-done.1 = bf16[768,1536]{1,0:T(8,128)(2,1)} collective-permute-done((bf16[768,1536]{1,0:T(8,128)(2,1)}, bf16[768,1536]{1,0:T(8,128)(2,1)}, u32[]{:S(2)}, u32[]{:S(2)}) %collective-permute-start.1) | collective-permute-done | bytes 2359328 | tf_op jit(solution)/shard_map/ppermute | solution.py:12
  314.3 3.9 copy-done
  318.2 3.6 copy-done.1
  321.8 158.6 %while.25 = (s32[]{:T(128)}, bf16[2,384,1536]{2,1,0:T(8,128)(2,1)}, s32[2]{0:T(128)S(1)}, bf16[2,384,1536]{2,1,0:T(8,128)(2,1)}, s32[2,7]{1,0:T(2,128)S(1)}, /*i...) while((s32[]{:T(128)}, bf16[2,384,1536]{2,1,0:T(8,128)(2,1)}, ...), condition=%wide.region_5.6_spmd, body=%wide.region_0.5_spmd.sunk | while | flops 535806272 | bytes 52914680 | solution.py:75
  324.4 9.2 %gather_fusion = bf16[7,384,1536]{2,1,0:T(8,128)(2,1)} fusion(bf16[10,384,1536]{2,1,0:T(8,128)(2,1)} %get-tuple-element.375, s32[1024]{0:T(1024)S(1)} %pad_clamp_fusion.2), kind=kCustom, calls=%fused_computation.clone.1 | custom fusion | bytes 16515100 | tf_op jit(solution)/shard_map/while/body/eval_jaxpr/gather | solution.py:44
  333.6 9.2 %gather_fusion.1 = bf16[7,384,1536]{2,1,0:T(8,128)(2,1)} fusion(bf16[10,384,1536]{2,1,0:T(8,128)(2,1)} %get-tuple-element.376, s32[1024]{0:T(1024)S(1)} %pad_clamp_fusion.2), kind=kCustom, calls=%fused_computation.1.clone.1 | custom fusion | bytes 16515100 | tf_op jit(solution)/shard_map/while/body/eval_jaxpr/gather | solution.py:45
  344.2 55.8 %while.26 = (s32[]{:T(128)}, bf16[384,1536]{1,0:T(8,128)(2,1)S(1)}, bf16[384,1536]{1,0:T(8,128)(2,1)S(1)}, bf16[2688,1536]{1,0:T(8,128)(2,1)}, bf16[2688,1536]{1...) while((s32[]{:T(128)}, bf16[384,1536]{1,0:T(8,128)(2,1)S(1)}, ...), condition=%wide.region_4.4_spmd.clone, body=%wide.region_1.3_spmd.clone.sunk | while | flops 535805184 | bytes 13981210 | solution.py:73
  353.6 1.9 fusion.34
  358.2 1.9 fusion.34
  362.9 1.9 fusion.34
  372.2 1.9 fusion.34
  376.9 1.9 fusion.34
  386.2 1.9 fusion.34
  390.8 1.9 fusion.34
  395.5 1.9 fusion.34
  403.7 9.2 %gather_fusion = bf16[7,384,1536]{2,1,0:T(8,128)(2,1)} fusion(bf16[10,384,1536]{2,1,0:T(8,128)(2,1)} %get-tuple-element.375, s32[1024]{0:T(1024)S(1)} %pad_clamp_fusion.2), kind=kCustom, calls=%fused_computation.clone.1 | custom fusion | bytes 16515100 | tf_op jit(solution)/shard_map/while/body/eval_jaxpr/gather | solution.py:44
  412.8 9.2 %gather_fusion.1 = bf16[7,384,1536]{2,1,0:T(8,128)(2,1)} fusion(bf16[10,384,1536]{2,1,0:T(8,128)(2,1)} %get-tuple-element.376, s32[1024]{0:T(1024)S(1)} %pad_clamp_fusion.2), kind=kCustom, calls=%fused_computation.1.clone.1 | custom fusion | bytes 16515100 | tf_op jit(solution)/shard_map/while/body/eval_jaxpr/gather | solution.py:45
  423.5 55.8 %while.26 = (s32[]{:T(128)}, bf16[384,1536]{1,0:T(8,128)(2,1)S(1)}, bf16[384,1536]{1,0:T(8,128)(2,1)S(1)}, bf16[2688,1536]{1,0:T(8,128)(2,1)}, bf16[2688,1536]{1...) while((s32[]{:T(128)}, bf16[384,1536]{1,0:T(8,128)(2,1)S(1)}, ...), condition=%wide.region_4.4_spmd.clone, body=%wide.region_1.3_spmd.clone.sunk | while | flops 535805184 | bytes 13981210 | solution.py:73
  423.6 1.9 fusion.34
  432.9 1.9 fusion.34
  437.5 1.9 fusion.34
  451.5 1.9 fusion.34
  456.1 1.9 fusion.34
  470.1 1.9 fusion.34
  474.7 1.9 fusion.34
  (147 shorter events, 106.0 us)
Async XLA Ops:
  0.0 257.7 %copy-start.3 = (bf16[768,1536]{1,0:T(8,128)(2,1)S(1)}, bf16[768,1536]{1,0:T(8,128)(2,1)}, u32[]{:S(2)}) copy-start(bf16[768,1536]{1,0:T(8,128)(2,1)} %param.9) | copy-start | bytes 7077892
  0.0 79.6 %collective-permute-start.4 = (bf16[768,1536]{1,0:T(8,128)(2,1)}, bf16[768,1536]{1,0:T(8,128)(2,1)}, u32[]{:S(2)}, u32[]{:S(2)}) collective-permute-start(bf16[768,1536]{1,0:T(8,128)(2,1)} %param.10), channel_id=1, source_target_pairs={{0,2},{1,3},{2,4},{3,5},{4,6},{5,7},{6,8},{7,9},{8,10},{9,11},{10,... | collective-permute-start | bytes 7077896 | tf_op jit(solution)/shard_map/ppermute | solution.py:12
  5.5 200.5 %collective-permute-start.5 = (bf16[768,1536]{1,0:T(8,128)(2,1)}, bf16[768,1536]{1,0:T(8,128)(2,1)}, u32[]{:S(2)}, u32[]{:S(2)}) collective-permute-start(bf16[768,1536]{1,0:T(8,128)(2,1)} %param.10), channel_id=1, source_target_pairs={{0,1},{1,2},{2,3},{3,4},{4,5},{5,6},{6,7},{7,8},{8,9},{9,10},{10,1... | collective-permute-start | bytes 7077896 | tf_op jit(solution)/shard_map/ppermute | solution.py:12
  8.1 249.6 %collective-permute-start = (bf16[768,1536]{1,0:T(8,128)(2,1)}, bf16[768,1536]{1,0:T(8,128)(2,1)}, u32[]{:S(2)}, u32[]{:S(2)}) collective-permute-start(bf16[768,1536]{1,0:T(8,128)(2,1)} %param.9), channel_id=1, source_target_pairs={{0,2},{1,3},{2,4},{3,5},{4,6},{5,7},{6,8},{7,9},{8,10},{9,11},{10,... | collective-permute-start | bytes 7077896 | tf_op jit(solution)/shard_map/ppermute | solution.py:12
  12.7 295.6 %collective-permute-start.1 = (bf16[768,1536]{1,0:T(8,128)(2,1)}, bf16[768,1536]{1,0:T(8,128)(2,1)}, u32[]{:S(2)}, u32[]{:S(2)}) collective-permute-start(bf16[768,1536]{1,0:T(8,128)(2,1)} %param.9), channel_id=1, source_target_pairs={{0,1},{1,2},{2,3},{3,4},{4,5},{5,6},{6,7},{7,8},{8,9},{9,10},{10,1... | collective-permute-start | bytes 7077896 | tf_op jit(solution)/shard_map/ppermute | solution.py:12
  14.6 295.7 %collective-permute-start.6 = (bf16[768,1536]{1,0:T(8,128)(2,1)}, bf16[768,1536]{1,0:T(8,128)(2,1)}, u32[]{:S(2)}, u32[]{:S(2)}) collective-permute-start(bf16[768,1536]{1,0:T(8,128)(2,1)} %param.10), channel_id=1, source_target_pairs={{1,0},{2,1},{3,2},{4,3},{5,4},{6,5},{7,6},{8,7},{9,8},{10,9},{11,1... | collective-permute-start | bytes 7077896 | tf_op jit(solution)/shard_map/ppermute | solution.py:12
  79.6 232.5 %collective-permute-start.7 = (bf16[768,1536]{1,0:T(8,128)(2,1)}, bf16[768,1536]{1,0:T(8,128)(2,1)}, u32[]{:S(2)}, u32[]{:S(2)}) collective-permute-start(bf16[768,1536]{1,0:T(8,128)(2,1)} %param.10), channel_id=1, source_target_pairs={{2,0},{3,1},{4,2},{5,3},{6,4},{7,5},{8,6},{9,7},{10,8},{11,9},{12,... | collective-permute-start | bytes 7077896 | tf_op jit(solution)/shard_map/ppermute | solution.py:12
  80.9 179.9 %copy-start.2 = (bf16[768,1536]{1,0:T(8,128)(2,1)S(1)}, bf16[768,1536]{1,0:T(8,128)(2,1)}, u32[]{:S(2)}) copy-start(bf16[768,1536]{1,0:T(8,128)(2,1)} %param.10) | copy-start | bytes 7077892
  206.0 107.9 %collective-permute-start.2 = (bf16[768,1536]{1,0:T(8,128)(2,1)}, bf16[768,1536]{1,0:T(8,128)(2,1)S(1)}, u32[]{:S(2)}, u32[]{:S(2)}) collective-permute-start(bf16[768,1536]{1,0:T(8,128)(2,1)} %param.9), channel_id=1, source_target_pairs={{1,0},{2,1},{3,2},{4,3},{5,4},{6,5},{7,6},{8,7},{9,8},{10,9},{11,1... | collective-permute-start | bytes 7077896 | tf_op jit(solution)/shard_map/ppermute | solution.py:12
  257.7 56.4 %collective-permute-start.3 = (bf16[768,1536]{1,0:T(8,128)(2,1)S(1)}, bf16[768,1536]{1,0:T(8,128)(2,1)S(1)}, u32[]{:S(2)}, u32[]{:S(2)}) collective-permute-start(bf16[768,1536]{1,0:T(8,128)(2,1)S(1)} %copy-done.3), channel_id=1, source_target_pairs={{2,0},{3,1},{4,2},{5,3},{6,4},{7,5},{8,6},{9,7},{10,8},{11,9},{12,... | collective-permute-start | bytes 7077896 | tf_op jit(solution)/shard_map/ppermute | solution.py:12
  313.9 4.3 copy-start
  313.9 7.9 %copy-start.4 = (s32[2,7]{1,0:T(2,128)S(1)}, s32[2,7]{1,0:T(2,128)}, u32[]{:S(2)}) copy-start(s32[2,7]{1,0:T(2,128)} %param.11) | copy-start | bytes 172
  314.3 7.5 %copy-start.1 = (bf16[3840,1536]{1,0:T(8,128)(2,1)}, bf16[3840,1536]{1,0:T(8,128)(2,1)S(1)}, u32[]{:S(2)}) copy-start(bf16[3840,1536]{1,0:T(8,128)(2,1)S(1)} %constant_dynamic-update-slice_fusion) | copy-start | bytes 35389444
where the time goes:
time: 483 us; the launch traced here: 480 us
  waiting for transfers between devices  280 us (58%)
  matrix products  91.9 us (19%)
  local copies, waits for them, and re-layouts  64.2 us (13%)
  starting transfers between devices  22.8 us (5%)
  other arithmetic  16.9 us (3%)
    ppermute x8, waiting for transfers between devices, passed_along(): lax.ppermute(value, axis, [(source, source + steps) for source in range(i...  280 us
    dot_general x24, matrix products, one_head(): lax.dot_general(query_cols, key_cols, (((1,), (1,)), ((), ())), preferred...  46.6 us
    dot_general x24, matrix products, one_head(): summed = jnp.dot(rounded, value_cols, preferred_element_type=jnp.float32)  45.3 us
    ppermute x8, starting transfers between devices, passed_along(): lax.ppermute(value, axis, [(source, source + steps) for source in range(i...  22.8 us
    gather x2, local copies, waits for them, and re-layouts, one_tile(): key_rows = window_keys[local].reshape(slots * tile_len, width)  18.4 us
    gather x2, local copies, waits for them, and re-layouts, one_tile(): value_rows = window_values[local].reshape(slots * tile_len, width)  18.3 us
    unnamed x18, local copies, waits for them, and re-layouts  17.1 us
    reduce_sum x24, other arithmetic, one_head(): total = jnp.sum(weights, axis=1, keepdims=True)  16.9 us
  transfers between devices with their start and end apart: 8, of which 4 were waited for; matrix products, arithmetic and copies ran while one was open for 2% of the time, Pallas kernels for 0%

commit v1 on v0

v1 whole, which is shorter than its diff:
```python
import functools

import jax
import jax.numpy as jnp
from jax import lax
from jax.experimental import pallas as pl
from jax.experimental.pallas import tpu as pltpu
from jax.sharding import PartitionSpec as P

HD = 128
LOG2E = 1.4426950408889634
SOURCES = 6
HEAD_US = 6


def heads_kernel(
    heads, first, slots, tile, table, place, q_ref, k_own, v_own, k_mate, v_mate, *rest
):
    far = rest[:4]
    out_ref, k_win, v_win, scores, sems = rest[-5:]
    step = pl.program_id(0)
    rows, hd = q_ref.shape
    tiles = rows // tile

    def copies(at, slot):
        col = pl.ds(pl.multiple_of((first + at) * hd, hd), hd)
        k_col = pl.ds(pl.multiple_of(at * hd, hd), hd)
        v_col = pl.ds(pl.multiple_of((heads + at) * hd, hd), hd)
        pairs = [(k_own.at[:, col], v_own.at[:, col])]
        pairs += [(k_mate.at[:, col], v_mate.at[:, col])]
        pairs += [(block.at[:, k_col], block.at[:, v_col]) for block in far]
        made = []
        for source, (k, v) in enumerate(pairs):
            where = pl.ds(pl.multiple_of(place[source] * rows, rows), rows)
            made.append(pltpu.make_async_copy(k, k_win.at[slot, where], sems.at[slot, source, 0]))
            made.append(pltpu.make_async_copy(v, v_win.at[slot, where], sems.at[slot, source, 1]))
        return made

    slot = lax.rem(step, 2)

    @pl.when(step == 0)
    def _():
        for copy in copies(0, 0):
            copy.start()

    @pl.when(step + 1 < heads)
    def _():
        for copy in copies(step + 1, 1 - slot):
            copy.start()

    for copy in copies(step, slot):
        copy.wait()

    factor = hd**-0.5 * LOG2E
    for t in range(tiles):
        valid = []
        starts = []
        for j in range(slots):
            named = table[t * slots + j]
            valid.append(named >= 0)
            starts.append(pl.multiple_of(jnp.maximum(named, 0) * tile, tile))
        q = q_ref[t * tile : (t + 1) * tile, :]
        peak = None
        for j in range(slots):
            k = k_win[slot, pl.ds(starts[j], tile), :]
            s = lax.dot_general(
                q, k, (((1,), (1,)), ((), ())), preferred_element_type=jnp.float32
            )
            s = s * factor
            scores[j] = s
            most = s[:, :128]
            for lane in range(128, tile, 128):
                most = jnp.maximum(most, s[:, lane : lane + 128])
            most = jnp.where(valid[j], most, -3e38)
            peak = most if peak is None else jnp.maximum(peak, most)
        peak = jnp.max(peak, axis=1, keepdims=True)
        total = None
        summed = None
        for j in range(slots):
            weights = jnp.exp2(scores[j] - jnp.where(valid[j], peak, 3e38))
            part = weights[:, :128]
            for lane in range(128, tile, 128):
                part = part + weights[:, lane : lane + 128]
            total = part if total is None else total + part
            v = v_win[slot, pl.ds(starts[j], tile), :]
            term = jnp.dot(weights.astype(jnp.bfloat16), v, preferred_element_type=jnp.float32)
            summed = term if summed is None else summed + term
        total = jnp.sum(total, axis=1, keepdims=True)
        out_ref[t * tile : (t + 1) * tile, :] = (summed / total).astype(out_ref.dtype)


def attend(first, heads, tile, table, place, queries, blocks, previous):
    rows, width = queries.shape
    slots = table.shape[0] // (rows // tile)
    anywhere = pl.BlockSpec(memory_space=pl.ANY)
    one_head = pl.BlockSpec((rows, HD), lambda step, *_: (0, first + step))
    operands = [table, place, queries, *blocks]
    specs = [one_head] + [anywhere] * len(blocks)
    aliases = {}
    if previous is not None:
        aliases = {len(operands): 0}
        operands.append(previous)
        specs.append(anywhere)
    return pl.pallas_call(
        functools.partial(heads_kernel, heads, first, slots, tile),
        out_shape=jax.ShapeDtypeStruct((rows, width), queries.dtype),
        grid_spec=pltpu.PrefetchScalarGridSpec(
            num_scalar_prefetch=2,
            grid=(heads,),
            in_specs=specs,
            out_specs=one_head,
            scratch_shapes=[
                pltpu.VMEM((2, SOURCES * rows, HD), queries.dtype),
                pltpu.VMEM((2, SOURCES * rows, HD), queries.dtype),
                pltpu.VMEM((slots, tile, tile), jnp.float32),
                pltpu.SemaphoreType.DMA((2, SOURCES, 2)),
            ],
        ),
        input_output_aliases=aliases,
        compiler_params=pltpu.CompilerParams(vmem_limit_bytes=40 * 1024 * 1024),
        cost_estimate=pl.CostEstimate(
            flops=4 * heads * rows * slots * tile * HD,
            bytes_accessed=heads * rows * HD * 2 * 14,
            transcendentals=heads * rows * slots * tile,
        ),
    )(*operands)


def head_cuts(head_count):
    return [2] * (head_count // 2) + [1] * (head_count % 2)


def on_device(queries, keys, values, neighbours):
    rows, width = queries.shape
    tiles = neighbours.shape[0]
    tile = rows // tiles
    count = lax.axis_size("blk")
    block = lax.axis_index("blk")
    cuts = head_cuts(width // HD)

    quads = range(0, count, 4)
    mates = [(b, b ^ 1) for b in range(count)]
    across = [(b, b ^ 2) for b in range(count)]
    onward = [(b, b + 4 if b % 4 < 2 else b - 4) for b in range(count)]
    onward = [(b, to) for b, to in onward if 0 <= to < count]
    pass_first = [pair for b in quads for pair in ((b, b + 1), (b + 3, b + 2))]
    pass_second = [pair for b in quads for pair in ((b + 1, b), (b + 2, b + 3))]

    place = jnp.array(
        [
            [2, 3, 4, 0, 5, 1],
            [2, 1, 4, 0, 3, 5],
            [2, 3, 0, 4, 1, 5],
            [2, 1, 0, 4, 5, 3],
        ],
        jnp.int32,
    )[lax.rem(block, 4)]
    base = (block - 2) * tiles
    table = jnp.where(neighbours >= 0, neighbours - base, -1).reshape(-1)

    k_mate = lax.ppermute(keys, "blk", mates)
    v_mate = lax.ppermute(values, "blk", mates)

    output = None
    first = 0
    crossed = []
    waiting = []
    for chunk, heads in enumerate(cuts):
        cols = slice(first * HD, (first + heads) * HD)
        k_part, v_part = keys[:, cols], values[:, cols]
        if chunk >= 2:
            k_part, v_part, crossed[chunk - 2] = lax.optimization_barrier(
                (k_part, v_part, crossed[chunk - 2])
            )
        packed = jnp.concatenate([k_part, v_part], axis=1)
        crossed.append(lax.ppermute(packed, "blk", across))
        first += heads
    first = 0
    for chunk, heads in enumerate(cuts):
        y = crossed[chunk]
        z = lax.ppermute(y, "blk", onward)
        y_pass = lax.ppermute(y, "blk", pass_first)
        z_pass = lax.ppermute(z, "blk", pass_second)
        blocks = (keys, values, k_mate, v_mate, y, z, y_pass, z_pass)
        output = attend(first, heads, tile, table, place, queries, blocks, output)
        first += heads
    return output


def solution(mesh):
    spec = P(("groups", "blk"), None)
    return jax.shard_map(
        on_device, mesh=mesh, in_specs=(spec,) * 4, out_specs=spec, check_vma=False
    )
```

time: 483 us -> 218 us (0.45)
  waiting for transfers between devices: 280 us -> 68.4 us
  matrix products: 91.9 us -> 0 us
  Pallas kernels: 0 us -> 62.9 us
  local copies, waits for them, and re-layouts: 64.2 us -> 16.2 us
  starting transfers between devices: 22.8 us -> 68.8 us
  other arithmetic: 16.9 us -> 0.33 us
    ppermute x8 -> x26, waiting for transfers between devices: 280 us -> 68.4 us  [the longest x6 49.3 us: on_device(): crossed.append(lax.ppermute(packed, 'blk', across))]
    dot_general x48 -> x0, matrix products: 91.9 us -> none  [the longest x24 46.6 us: one_head(): lax.dot_general(query_cols, key_cols, (((1,), (1,)), ((), ())), preferred...]
    pallas_call x0 -> x6, Pallas kernels: none -> 62.9 us  [attend(): pl.pallas_call(functools.partial(heads_kernel, heads, first, slots, tile)...]
    ppermute x8 -> x26, starting transfers between devices: 22.8 us -> 68.8 us  [the longest x6 26.1 us: on_device(): z_pass = lax.ppermute(z, 'blk', pass_second)]
    gather x4 -> x0, local copies, waits for them, and re-layouts: 36.7 us -> none  [the longest x2 18.4 us: one_tile(): key_rows = window_keys[local].reshape(slots * tile_len, width)]
    reduce_sum x24 -> x0, other arithmetic: 16.9 us -> none  [one_head(): total = jnp.sum(weights, axis=1, keepdims=True)]
    unnamed x18 -> x52, local copies, waits for them, and re-layouts: 17.1 us -> 13.3 us
  transfers between devices with their start and end apart: 8 -> 26, of which waited for: 4 -> 9; matrix products, arithmetic and copies ran while one was open for 2% -> 0% of each run, Pallas kernels for 0% -> 24%
where the time goes in v1:
time: 218 us; the launch traced here: 217 us
  starting transfers between devices  68.8 us (32%)
  waiting for transfers between devices  68.4 us (31%)
  Pallas kernels  62.9 us (29%)
  local copies, waits for them, and re-layouts  16.2 us (7%)
    pallas_call x6, Pallas kernels, attend(): pl.pallas_call(functools.partial(heads_kernel, heads, first, slots, tile)...  62.9 us
    ppermute x6, waiting for transfers between devices, on_device(): crossed.append(lax.ppermute(packed, 'blk', across))  49.3 us
    ppermute x6, starting transfers between devices, on_device(): z_pass = lax.ppermute(z, 'blk', pass_second)  26.1 us
    ppermute x6, starting transfers between devices, on_device(): z = lax.ppermute(y, 'blk', onward)  20.5 us
    ppermute x6, waiting for transfers between devices, on_device(): z = lax.ppermute(y, 'blk', onward)  19.1 us
    unnamed x52, local copies, waits for them, and re-layouts  13.3 us
    ppermute x6, starting transfers between devices, on_device(): crossed.append(lax.ppermute(packed, 'blk', across))  11.2 us
    ppermute x6, starting transfers between devices, on_device(): y_pass = lax.ppermute(y, 'blk', pass_first)  7.84 us
  transfers between devices with their start and end apart: 26, of which 9 were waited for; matrix products, arithmetic and copies ran while one was open for 0% of the time, Pallas kernels for 24%

profile of v1, /device:TPU:1, one launch (start us, length us, event | category | flops | bytes accessed | tf_op | source)
XLA Modules:
  0.0 217.3 jit_solution(7392328765860455333)
XLA Ops:
  0.0 1.9 fusion
  2.6 2.1 collective-permute-start.8
  4.9 17.1 %collective-permute-done.8.rest_0_ = bf16[768,512]{1,0:T(8,128)(2,1)S(1)} collective-permute-done((bf16[768,512]{1,0:T(8,128)(2,1)S(1)}, bf16[768,512]{1,0:T(8,128)(2,1)S(1)}, u32[]{:S(2)}, u32[]{:S(2)}) %collective-permute-start.8) | collective-permute-done | bytes 786464 | tf_op jit(solution)/shard_map/ppermute | solution.py:176
  22.0 3.1 %collective-permute-start.23 = (bf16[768,512]{1,0:T(8,128)(2,1)S(1)}, bf16[768,512]{1,0:T(8,128)(2,1)S(1)}, u32[]{:S(2)}, u32[]{:S(2)}) collective-permute-start(bf16[768,512]{1,0:T(8,128)(2,1)S(1)} %collective-permute-done.8.rest_0_), channel_id=1, source_target_pairs={{0,4},{1,5},{4,8},{5,9},{6,2},{7,3},{8,12},{9,13},{10,6},{11,7},{1... | collective-permute-start | bytes 2359304 | tf_op jit(solution)/shard_map/ppermute | solution.py:181
  25.2 3.0 %collective-permute-start = (bf16[768,1536]{1,0:T(8,128)(2,1)S(1)}, bf16[768,1536]{1,0:T(8,128)(2,1)S(1)}, u32[]{:S(2)}, u32[]{:S(2)}) collective-permute-start(bf16[768,1536]{1,0:T(8,128)(2,1)S(1)} %copy-done), channel_id=1, source_target_pairs={{0,1},{1,0},{2,3},{3,2},{4,5},{5,4},{6,7},{7,6},{8,9},{9,8},{10,11... | collective-permute-start | bytes 7077896 | tf_op jit(solution)/shard_map/ppermute | solution.py:161
  29.6 9.3 %collective-permute-done.2.rest_0_ = bf16[768,512]{1,0:T(8,128)(2,1)S(1)} collective-permute-done((bf16[768,512]{1,0:T(8,128)(2,1)S(1)}, bf16[768,512]{1,0:T(8,128)(2,1)S(1)}, u32[]{:S(2)}, u32[]{:S(2)}) %collective-permute-start.2) | collective-permute-done | bytes 786464 | tf_op jit(solution)/shard_map/ppermute | solution.py:176
  38.9 3.1 %collective-permute-start.20 = (bf16[768,512]{1,0:T(8,128)(2,1)S(1)}, bf16[768,512]{1,0:T(8,128)(2,1)S(1)}, u32[]{:S(2)}, u32[]{:S(2)}) collective-permute-start(bf16[768,512]{1,0:T(8,128)(2,1)S(1)} %collective-permute-done.2.rest_0_), channel_id=1, source_target_pairs={{0,4},{1,5},{4,8},{5,9},{6,2},{7,3},{8,12},{9,13},{10,6},{11,7},{1... | collective-permute-start | bytes 2359304 | tf_op jit(solution)/shard_map/ppermute | solution.py:181
  43.5 3.7 %collective-permute-start.9 = (bf16[768,512]{1,0:T(8,128)(2,1)S(1)}, bf16[768,512]{1,0:T(8,128)(2,1)S(1)}, u32[]{:S(2)}, u32[]{:S(2)}) collective-permute-start(bf16[768,512]{1,0:T(8,128)(2,1)S(1)} %pad_maximum_fusion.4), channel_id=1, source_target_pairs={{0,2},{1,3},{2,0},{3,1},{4,6},{5,7},{6,4},{7,5},{8,10},{9,11},{10,... | collective-permute-start | bytes 2359304 | tf_op jit(solution)/shard_map/ppermute | solution.py:176
  47.2 10.1 %collective-permute-done.20.rest_1_ = bf16[768,512]{1,0:T(8,128)(2,1)S(1)} collective-permute-done((bf16[768,512]{1,0:T(8,128)(2,1)S(1)}, bf16[768,512]{1,0:T(8,128)(2,1)S(1)}, u32[]{:S(2)}, u32[]{:S(2)}) %collective-permute-start.20) | collective-permute-done | bytes 786464 | tf_op jit(solution)/shard_map/ppermute | solution.py:181
  57.3 2.1 collective-permute-start.3
  59.4 4.7 %collective-permute-start.25 = (bf16[768,512]{1,0:T(8,128)(2,1)S(1)}, bf16[768,512]{1,0:T(8,128)(2,1)S(1)}, u32[]{:S(2)}, u32[]{:S(2)}) collective-permute-start(bf16[768,512]{1,0:T(8,128)(2,1)S(1)} %collective-permute-done.23.rest_1_), channel_id=1, source_target_pairs={{1,0},{2,3},{5,4},{6,7},{9,8},{10,11},{13,12},{14,15},{17,16},{18,... | collective-permute-start | bytes 2359304 | tf_op jit(solution)/shard_map/ppermute | solution.py:183
  65.0 2.7 %collective-permute-start.22 = (bf16[768,512]{1,0:T(8,128)(2,1)S(1)}, bf16[768,512]{1,0:T(8,128)(2,1)S(1)}, u32[]{:S(2)}, u32[]{:S(2)}) collective-permute-start(bf16[768,512]{1,0:T(8,128)(2,1)S(1)} %collective-permute-done.20.rest_1_), channel_id=1, source_target_pairs={{1,0},{2,3},{5,4},{6,7},{9,8},{10,11},{13,12},{14,15},{17,16},{18,... | collective-permute-start | bytes 2359304 | tf_op jit(solution)/shard_map/ppermute | solution.py:183
  67.8 14.2 %collective-permute-done.3.rest_0_ = bf16[768,512]{1,0:T(8,128)(2,1)} collective-permute-done((bf16[768,512]{1,0:T(8,128)(2,1)S(1)}, bf16[768,512]{1,0:T(8,128)(2,1)}, u32[]{:S(2)}, u32[]{:S(2)}) %collective-permute-start.3) | collective-permute-done | bytes 786464 | tf_op jit(solution)/shard_map/ppermute | solution.py:176
  82.0 4.1 %collective-permute-start.17 = (bf16[768,512]{1,0:T(8,128)(2,1)S(1)}, bf16[768,512]{1,0:T(8,128)(2,1)}, u32[]{:S(2)}, u32[]{:S(2)}) collective-permute-start(bf16[768,512]{1,0:T(8,128)(2,1)S(1)} %collective-permute-done.9.rest_0_), channel_id=1, source_target_pairs={{0,4},{1,5},{4,8},{5,9},{6,2},{7,3},{8,12},{9,13},{10,6},{11,7},{1... | collective-permute-start | bytes 2359304 | tf_op jit(solution)/shard_map/ppermute | solution.py:181
  89.0 3.2 %collective-permute-start.4 = (bf16[768,512]{1,0:T(8,128)(2,1)S(1)}, bf16[768,512]{1,0:T(8,128)(2,1)}, u32[]{:S(2)}, u32[]{:S(2)}) collective-permute-start(bf16[768,512]{1,0:T(8,128)(2,1)S(1)} %pad_maximum_fusion.2), channel_id=1, source_target_pairs={{0,2},{1,3},{2,0},{3,1},{4,6},{5,7},{6,4},{7,5},{8,10},{9,11},{10,... | collective-permute-start | bytes 2359304 | tf_op jit(solution)/shard_map/ppermute | solution.py:176
  93.2 3.3 %collective-permute-start.14 = (bf16[768,512]{1,0:T(8,128)(2,1)}, bf16[768,512]{1,0:T(8,128)(2,1)}, u32[]{:S(2)}, u32[]{:S(2)}) collective-permute-start(bf16[768,512]{1,0:T(8,128)(2,1)} %collective-permute-done.3.rest_0_), channel_id=1, source_target_pairs={{0,4},{1,5},{4,8},{5,9},{6,2},{7,3},{8,12},{9,13},{10,6},{11,7},{1... | collective-permute-start | bytes 2359304 | tf_op jit(solution)/shard_map/ppermute | solution.py:181
  96.5 5.1 %collective-permute-done.17.rest_1_ = bf16[768,512]{1,0:T(8,128)(2,1)} collective-permute-done((bf16[768,512]{1,0:T(8,128)(2,1)S(1)}, bf16[768,512]{1,0:T(8,128)(2,1)}, u32[]{:S(2)}, u32[]{:S(2)}) %collective-permute-start.17) | collective-permute-done | bytes 786464 | tf_op jit(solution)/shard_map/ppermute | solution.py:181
  104.5 3.5 %collective-permute-start.11 = (bf16[768,512]{1,0:T(8,128)(2,1)}, bf16[768,512]{1,0:T(8,128)(2,1)}, u32[]{:S(2)}, u32[]{:S(2)}) collective-permute-start(bf16[768,512]{1,0:T(8,128)(2,1)} %collective-permute-done.10.rest_0_), channel_id=1, source_target_pairs={{0,4},{1,5},{4,8},{5,9},{6,2},{7,3},{8,12},{9,13},{10,6},{11,7},{1... | collective-permute-start | bytes 2359304 | tf_op jit(solution)/shard_map/ppermute | solution.py:181
  108.9 6.3 %collective-permute-start.19 = (bf16[768,512]{1,0:T(8,128)(2,1)}, bf16[768,512]{1,0:T(8,128)(2,1)}, u32[]{:S(2)}, u32[]{:S(2)}) collective-permute-start(bf16[768,512]{1,0:T(8,128)(2,1)} %collective-permute-done.17.rest_1_), channel_id=1, source_target_pairs={{1,0},{2,3},{5,4},{6,7},{9,8},{10,11},{13,12},{14,15},{17,16},{18,... | collective-permute-start | bytes 2359304 | tf_op jit(solution)/shard_map/ppermute | solution.py:183
  115.2 6.2 %collective-permute-done.4.rest_0_ = bf16[768,512]{1,0:T(8,128)(2,1)} collective-permute-done((bf16[768,512]{1,0:T(8,128)(2,1)S(1)}, bf16[768,512]{1,0:T(8,128)(2,1)}, u32[]{:S(2)}, u32[]{:S(2)}) %collective-permute-start.4) | collective-permute-done | bytes 786464 | tf_op jit(solution)/shard_map/ppermute | solution.py:176
  121.4 3.3 %collective-permute-start.5 = (bf16[768,512]{1,0:T(8,128)(2,1)}, bf16[768,512]{1,0:T(8,128)(2,1)}, u32[]{:S(2)}, u32[]{:S(2)}) collective-permute-start(bf16[768,512]{1,0:T(8,128)(2,1)} %collective-permute-done.4.rest_0_), channel_id=1, source_target_pairs={{0,4},{1,5},{4,8},{5,9},{6,2},{7,3},{8,12},{9,13},{10,6},{11,7},{1... | collective-permute-start | bytes 2359304 | tf_op jit(solution)/shard_map/ppermute | solution.py:181
  124.6 4.8 %collective-permute-start.16 = (bf16[768,512]{1,0:T(8,128)(2,1)}, bf16[768,512]{1,0:T(8,128)(2,1)}, u32[]{:S(2)}, u32[]{:S(2)}) collective-permute-start(bf16[768,512]{1,0:T(8,128)(2,1)} %collective-permute-done.14.rest_1_), channel_id=1, source_target_pairs={{1,0},{2,3},{5,4},{6,7},{9,8},{10,11},{13,12},{14,15},{17,16},{18,... | collective-permute-start | bytes 2359304 | tf_op jit(solution)/shard_map/ppermute | solution.py:183
  131.5 3.9 %collective-permute-done.11.rest_1_ = bf16[768,512]{1,0:T(8,128)(2,1)} collective-permute-done((bf16[768,512]{1,0:T(8,128)(2,1)}, bf16[768,512]{1,0:T(8,128)(2,1)}, u32[]{:S(2)}, u32[]{:S(2)}) %collective-permute-start.11) | collective-permute-done | bytes 786464 | tf_op jit(solution)/shard_map/ppermute | solution.py:181
  135.4 4.3 %collective-permute-start.13 = (bf16[768,512]{1,0:T(8,128)(2,1)}, bf16[768,512]{1,0:T(8,128)(2,1)S(1)}, u32[]{:S(2)}, u32[]{:S(2)}) collective-permute-start(bf16[768,512]{1,0:T(8,128)(2,1)} %collective-permute-done.11.rest_1_), channel_id=1, source_target_pairs={{1,0},{2,3},{5,4},{6,7},{9,8},{10,11},{13,12},{14,15},{17,16},{18,... | collective-permute-start | bytes 2359304 | tf_op jit(solution)/shard_map/ppermute | solution.py:183
  141.4 1.7 copy-done.3
  149.3 10.1 %shard_map.55.rest_4_ = bf16[768,1536]{1,0:T(8,128)(2,1)} custom-call(s32[14]{0:T(128)S(1)} %reshape.3.table, s32[6]{0:T(128)S(1)} %dynamic-slice_bitcast_fusion.place, bf16[768,1536]{1,0:T(8,128)(2,1)S(1)} %copy-done.3, bf16[768,1536]{1,0:T(8,128)(2,1)S(1)} %copy-done, bf16[768,1536]{1,0:T(8,128)(2,1)S(1)} %copy-done.2, bf16[768,1536]{1,0:T(8,128)(2,1)S(1)} %copy-done.5, ...), custom_call_target="tpu_custom_call" | custom-call | flops 2113929216 | bytes 5505024 | tf_op jit(solution)/shard_map/pallas_call | solution.py:104
  160.9 3.3 %collective-permute-start.7 = (bf16[768,512]{1,0:T(8,128)(2,1)}, bf16[768,512]{1,0:T(8,128)(2,1)S(1)}, u32[]{:S(2)}, u32[]{:S(2)}) collective-permute-start(bf16[768,512]{1,0:T(8,128)(2,1)} %collective-permute-done.5.rest_1_), channel_id=1, source_target_pairs={{1,0},{2,3},{5,4},{6,7},{9,8},{10,11},{13,12},{14,15},{17,16},{18,... | collective-permute-start | bytes 2359304 | tf_op jit(solution)/shard_map/ppermute | solution.py:183
  164.2 10.1 %shard_map.56.rest_4_ = bf16[768,1536]{1,0:T(8,128)(2,1)} custom-call(s32[14]{0:T(128)S(1)} %reshape.3.table, s32[6]{0:T(128)S(1)} %dynamic-slice_bitcast_fusion.place, bf16[768,1536]{1,0:T(8,128)(2,1)S(1)} %copy-done.3, bf16[768,1536]{1,0:T(8,128)(2,1)S(1)} %copy-done, bf16[768,1536]{1,0:T(8,128)(2,1)S(1)} %copy-done.2, ...), custom_call_target="tpu_custom_call", output_to_operand_aliasing={{}: (11, {})} | custom-call | flops 2113929216 | bytes 5505024 | tf_op jit(solution)/shard_map/pallas_call | solution.py:104
  174.3 10.5 %shard_map.57.rest_4_ = bf16[768,1536]{1,0:T(8,128)(2,1)} custom-call(s32[14]{0:T(128)S(1)} %reshape.3.table, s32[6]{0:T(128)S(1)} %dynamic-slice_bitcast_fusion.place, bf16[768,1536]{1,0:T(8,128)(2,1)S(1)} %copy-done.3, bf16[768,1536]{1,0:T(8,128)(2,1)S(1)} %copy-done, bf16[768,1536]{1,0:T(8,128)(2,1)S(1)} %copy-done.2, ...), custom_call_target="tpu_custom_call", output_to_operand_aliasing={{}: (11, {})} | custom-call | flops 2113929216 | bytes 5505024 | tf_op jit(solution)/shard_map/pallas_call | solution.py:104
  184.9 11.0 %shard_map.58.rest_4_ = bf16[768,1536]{1,0:T(8,128)(2,1)} custom-call(s32[14]{0:T(128)S(1)} %reshape.3.table, s32[6]{0:T(128)S(1)} %dynamic-slice_bitcast_fusion.place, bf16[768,1536]{1,0:T(8,128)(2,1)S(1)} %copy-done.3, bf16[768,1536]{1,0:T(8,128)(2,1)S(1)} %copy-done, bf16[768,1536]{1,0:T(8,128)(2,1)S(1)} %copy-done.2, ...), custom_call_target="tpu_custom_call", output_to_operand_aliasing={{}: (11, {})} | custom-call | flops 2113929216 | bytes 5505024 | tf_op jit(solution)/shard_map/pallas_call | solution.py:104
  195.9 10.5 %shard_map.59.rest_4_ = bf16[768,1536]{1,0:T(8,128)(2,1)} custom-call(s32[14]{0:T(128)S(1)} %reshape.3.table, s32[6]{0:T(128)S(1)} %dynamic-slice_bitcast_fusion.place, bf16[768,1536]{1,0:T(8,128)(2,1)S(1)} %copy-done.3, bf16[768,1536]{1,0:T(8,128)(2,1)S(1)} %copy-done, bf16[768,1536]{1,0:T(8,128)(2,1)S(1)} %copy-done.2, ...), custom_call_target="tpu_custom_call", output_to_operand_aliasing={{}: (11, {})} | custom-call | flops 2113929216 | bytes 5505024 | tf_op jit(solution)/shard_map/pallas_call | solution.py:104
  206.4 10.7 %shard_map.60 = bf16[768,1536]{1,0:T(8,128)(2,1)} custom-call(s32[14]{0:T(128)S(1)} %reshape.3.table, s32[6]{0:T(128)S(1)} %dynamic-slice_bitcast_fusion.place, bf16[768,1536]{1,0:T(8,128)(2,1)S(1)} %copy-done.3, bf16[768,1536]{1,0:T(8,128)(2,1)S(1)} %copy-done, bf16[768,1536]{1,0:T(8,128)(2,1)S(1)} %copy-done.2, ...), custom_call_target="tpu_custom_call", output_to_operand_aliasing={{}: (11, {})} | custom-call | flops 2113929216 | bytes 5505024 | tf_op jit(solution)/shard_map/pallas_call | solution.py:104
  (89 shorter events, 23.5 us)
Async XLA Ops:
  2.6 19.4 %collective-permute-start.8 = (bf16[768,512]{1,0:T(8,128)(2,1)S(1)}, bf16[768,512]{1,0:T(8,128)(2,1)S(1)}, u32[]{:S(2)}, u32[]{:S(2)}) collective-permute-start(bf16[768,512]{1,0:T(8,128)(2,1)S(1)} %pad_maximum_fusion.3), channel_id=1, source_target_pairs={{0,2},{1,3},{2,0},{3,1},{4,6},{5,7},{6,4},{7,5},{8,10},{9,11},{10,... | collective-permute-start | bytes 2359304 | tf_op jit(solution)/shard_map/ppermute | solution.py:176
  4.8 34.1 %collective-permute-start.2 = (bf16[768,512]{1,0:T(8,128)(2,1)S(1)}, bf16[768,512]{1,0:T(8,128)(2,1)S(1)}, u32[]{:S(2)}, u32[]{:S(2)}) collective-permute-start(bf16[768,512]{1,0:T(8,128)(2,1)S(1)} %pad_maximum_fusion), channel_id=1, source_target_pairs={{0,2},{1,3},{2,0},{3,1},{4,6},{5,7},{6,4},{7,5},{8,10},{9,11},{10,... | collective-permute-start | bytes 2359304 | tf_op jit(solution)/shard_map/ppermute | solution.py:176
  22.0 25.1 %copy-start.6 = (bf16[768,512]{1,0:T(8,128)(2,1)}, bf16[768,512]{1,0:T(8,128)(2,1)S(1)}, u32[]{:S(2)}) copy-start(bf16[768,512]{1,0:T(8,128)(2,1)S(1)} %collective-permute-done.8.rest_0_) | copy-start | bytes 2359300
  22.0 20.0 %collective-permute-start.23 = (bf16[768,512]{1,0:T(8,128)(2,1)S(1)}, bf16[768,512]{1,0:T(8,128)(2,1)S(1)}, u32[]{:S(2)}, u32[]{:S(2)}) collective-permute-start(bf16[768,512]{1,0:T(8,128)(2,1)S(1)} %collective-permute-done.8.rest_0_), channel_id=1, source_target_pairs={{0,4},{1,5},{4,8},{5,9},{6,2},{7,3},{8,12},{9,13},{10,6},{11,7},{1... | collective-permute-start | bytes 2359304 | tf_op jit(solution)/shard_map/ppermute | solution.py:181
  25.2 61.0 %collective-permute-start = (bf16[768,1536]{1,0:T(8,128)(2,1)S(1)}, bf16[768,1536]{1,0:T(8,128)(2,1)S(1)}, u32[]{:S(2)}, u32[]{:S(2)}) collective-permute-start(bf16[768,1536]{1,0:T(8,128)(2,1)S(1)} %copy-done), channel_id=1, source_target_pairs={{0,1},{1,0},{2,3},{3,2},{4,5},{5,4},{6,7},{7,6},{8,9},{9,8},{10,11... | collective-permute-start | bytes 7077896 | tf_op jit(solution)/shard_map/ppermute | solution.py:161
  28.2 60.8 %collective-permute-start.1 = (bf16[768,1536]{1,0:T(8,128)(2,1)S(1)}, bf16[768,1536]{1,0:T(8,128)(2,1)S(1)}, u32[]{:S(2)}, u32[]{:S(2)}) collective-permute-start(bf16[768,1536]{1,0:T(8,128)(2,1)S(1)} %copy-done.1), channel_id=1, source_target_pairs={{0,1},{1,0},{2,3},{3,2},{4,5},{5,4},{6,7},{7,6},{8,9},{9,8},{10,11... | collective-permute-start | bytes 7077896 | tf_op jit(solution)/shard_map/ppermute | solution.py:162
  28.3 15.1 %collective-permute-start.24 = (bf16[768,512]{1,0:T(8,128)(2,1)S(1)}, bf16[768,512]{1,0:T(8,128)(2,1)S(1)}, u32[]{:S(2)}, u32[]{:S(2)}) collective-permute-start(bf16[768,512]{1,0:T(8,128)(2,1)S(1)} %collective-permute-done.8.rest_0_), channel_id=1, source_target_pairs={{0,1},{3,2},{4,5},{7,6},{8,9},{11,10},{12,13},{15,14},{16,17},{19,... | collective-permute-start | bytes 2359304 | tf_op jit(solution)/shard_map/ppermute | solution.py:182
  38.9 18.4 %collective-permute-start.20 = (bf16[768,512]{1,0:T(8,128)(2,1)S(1)}, bf16[768,512]{1,0:T(8,128)(2,1)S(1)}, u32[]{:S(2)}, u32[]{:S(2)}) collective-permute-start(bf16[768,512]{1,0:T(8,128)(2,1)S(1)} %collective-permute-done.2.rest_0_), channel_id=1, source_target_pairs={{0,4},{1,5},{4,8},{5,9},{6,2},{7,3},{8,12},{9,13},{10,6},{11,7},{1... | collective-permute-start | bytes 2359304 | tf_op jit(solution)/shard_map/ppermute | solution.py:181
  42.1 17.4 %collective-permute-start.21 = (bf16[768,512]{1,0:T(8,128)(2,1)S(1)}, bf16[768,512]{1,0:T(8,128)(2,1)S(1)}, u32[]{:S(2)}, u32[]{:S(2)}) collective-permute-start(bf16[768,512]{1,0:T(8,128)(2,1)S(1)} %collective-permute-done.2.rest_0_), channel_id=1, source_target_pairs={{0,1},{3,2},{4,5},{7,6},{8,9},{11,10},{12,13},{15,14},{16,17},{19,... | collective-permute-start | bytes 2359304 | tf_op jit(solution)/shard_map/ppermute | solution.py:182
  43.4 24.4 %copy-start.14 = (bf16[768,512]{1,0:T(8,128)(2,1)}, bf16[768,512]{1,0:T(8,128)(2,1)S(1)}, u32[]{:S(2)}) copy-start(bf16[768,512]{1,0:T(8,128)(2,1)S(1)} %collective-permute-done.24.rest_2_) | copy-start | bytes 2359300
  43.5 21.6 %collective-permute-start.9 = (bf16[768,512]{1,0:T(8,128)(2,1)S(1)}, bf16[768,512]{1,0:T(8,128)(2,1)S(1)}, u32[]{:S(2)}, u32[]{:S(2)}) collective-permute-start(bf16[768,512]{1,0:T(8,128)(2,1)S(1)} %pad_maximum_fusion.4), channel_id=1, source_target_pairs={{0,2},{1,3},{2,0},{3,1},{4,6},{5,7},{6,4},{7,5},{8,10},{9,11},{10,... | collective-permute-start | bytes 2359304 | tf_op jit(solution)/shard_map/ppermute | solution.py:176
  57.3 28.9 %copy-start.10 = (bf16[768,512]{1,0:T(8,128)(2,1)}, bf16[768,512]{1,0:T(8,128)(2,1)S(1)}, u32[]{:S(2)}) copy-start(bf16[768,512]{1,0:T(8,128)(2,1)S(1)} %collective-permute-done.20.rest_1_) | copy-start | bytes 2359300
  57.3 24.7 %collective-permute-start.3 = (bf16[768,512]{1,0:T(8,128)(2,1)S(1)}, bf16[768,512]{1,0:T(8,128)(2,1)}, u32[]{:S(2)}, u32[]{:S(2)}) collective-permute-start(bf16[768,512]{1,0:T(8,128)(2,1)S(1)} %pad_maximum_fusion.1), channel_id=1, source_target_pairs={{0,2},{1,3},{2,0},{3,1},{4,6},{5,7},{6,4},{7,5},{8,10},{9,11},{10,... | collective-permute-start | bytes 2359304 | tf_op jit(solution)/shard_map/ppermute | solution.py:176
  59.4 26.8 %copy-start.12 = (bf16[768,512]{1,0:T(8,128)(2,1)}, bf16[768,512]{1,0:T(8,128)(2,1)S(1)}, u32[]{:S(2)}) copy-start(bf16[768,512]{1,0:T(8,128)(2,1)S(1)} %collective-permute-done.21.rest_2_) | copy-start | bytes 2359300
  59.4 26.7 %collective-permute-start.25 = (bf16[768,512]{1,0:T(8,128)(2,1)S(1)}, bf16[768,512]{1,0:T(8,128)(2,1)S(1)}, u32[]{:S(2)}, u32[]{:S(2)}) collective-permute-start(bf16[768,512]{1,0:T(8,128)(2,1)S(1)} %collective-permute-done.23.rest_1_), channel_id=1, source_target_pairs={{1,0},{2,3},{5,4},{6,7},{9,8},{10,11},{13,12},{14,15},{17,16},{18,... | collective-permute-start | bytes 2359304 | tf_op jit(solution)/shard_map/ppermute | solution.py:183
  65.0 27.2 %collective-permute-start.22 = (bf16[768,512]{1,0:T(8,128)(2,1)S(1)}, bf16[768,512]{1,0:T(8,128)(2,1)S(1)}, u32[]{:S(2)}, u32[]{:S(2)}) collective-permute-start(bf16[768,512]{1,0:T(8,128)(2,1)S(1)} %collective-permute-done.20.rest_1_), channel_id=1, source_target_pairs={{1,0},{2,3},{5,4},{6,7},{9,8},{10,11},{13,12},{14,15},{17,16},{18,... | collective-permute-start | bytes 2359304 | tf_op jit(solution)/shard_map/ppermute | solution.py:183
  67.8 61.7 %copy-start.25 = (s32[2,7]{1,0:T(2,128)S(1)}, s32[2,7]{1,0:T(2,128)}, u32[]{:S(2)}) copy-start(s32[2,7]{1,0:T(2,128)} %param.8) | copy-start | bytes 172
  82.0 19.6 %collective-permute-start.17 = (bf16[768,512]{1,0:T(8,128)(2,1)S(1)}, bf16[768,512]{1,0:T(8,128)(2,1)}, u32[]{:S(2)}, u32[]{:S(2)}) collective-permute-start(bf16[768,512]{1,0:T(8,128)(2,1)S(1)} %collective-permute-done.9.rest_0_), channel_id=1, source_target_pairs={{0,4},{1,5},{4,8},{5,9},{6,2},{7,3},{8,12},{9,13},{10,6},{11,7},{1... | collective-permute-start | bytes 2359304 | tf_op jit(solution)/shard_map/ppermute | solution.py:181
  86.1 18.4 %collective-permute-start.10 = (bf16[768,512]{1,0:T(8,128)(2,1)S(1)}, bf16[768,512]{1,0:T(8,128)(2,1)}, u32[]{:S(2)}, u32[]{:S(2)}) collective-permute-start(bf16[768,512]{1,0:T(8,128)(2,1)S(1)} %pad_maximum_fusion.5), channel_id=1, source_target_pairs={{0,2},{1,3},{2,0},{3,1},{4,6},{5,7},{6,4},{7,5},{8,10},{9,11},{10,... | collective-permute-start | bytes 2359304 | tf_op jit(solution)/shard_map/ppermute | solution.py:176
  87.7 20.3 %collective-permute-start.18 = (bf16[768,512]{1,0:T(8,128)(2,1)S(1)}, bf16[768,512]{1,0:T(8,128)(2,1)S(1)}, u32[]{:S(2)}, u32[]{:S(2)}) collective-permute-start(bf16[768,512]{1,0:T(8,128)(2,1)S(1)} %collective-permute-done.9.rest_0_), channel_id=1, source_target_pairs={{0,1},{3,2},{4,5},{7,6},{8,9},{11,10},{12,13},{15,14},{16,17},{19,... | collective-permute-start | bytes 2359304 | tf_op jit(solution)/shard_map/ppermute | solution.py:182
  89.0 26.1 %copy-start.24 = (bf16[768,1536]{1,0:T(8,128)(2,1)}, bf16[768,1536]{1,0:T(8,128)(2,1)S(1)}, u32[]{:S(2)}) copy-start(bf16[768,1536]{1,0:T(8,128)(2,1)S(1)} %collective-permute-done.1.v_mate) | copy-start | bytes 7077892
  89.0 32.3 %collective-permute-start.4 = (bf16[768,512]{1,0:T(8,128)(2,1)S(1)}, bf16[768,512]{1,0:T(8,128)(2,1)}, u32[]{:S(2)}, u32[]{:S(2)}) collective-permute-start(bf16[768,512]{1,0:T(8,128)(2,1)S(1)} %pad_maximum_fusion.2), channel_id=1, source_target_pairs={{0,2},{1,3},{2,0},{3,1},{4,6},{5,7},{6,4},{7,5},{8,10},{9,11},{10,... | collective-permute-start | bytes 2359304 | tf_op jit(solution)/shard_map/ppermute | solution.py:176
  93.2 31.5 %collective-permute-start.14 = (bf16[768,512]{1,0:T(8,128)(2,1)}, bf16[768,512]{1,0:T(8,128)(2,1)}, u32[]{:S(2)}, u32[]{:S(2)}) collective-permute-start(bf16[768,512]{1,0:T(8,128)(2,1)} %collective-permute-done.3.rest_0_), channel_id=1, source_target_pairs={{0,4},{1,5},{4,8},{5,9},{6,2},{7,3},{8,12},{9,13},{10,6},{11,7},{1... | collective-permute-start | bytes 2359304 | tf_op jit(solution)/shard_map/ppermute | solution.py:181
  101.6 28.6 %collective-permute-start.15 = (bf16[768,512]{1,0:T(8,128)(2,1)}, bf16[768,512]{1,0:T(8,128)(2,1)}, u32[]{:S(2)}, u32[]{:S(2)}) collective-permute-start(bf16[768,512]{1,0:T(8,128)(2,1)} %collective-permute-done.3.rest_0_), channel_id=1, source_target_pairs={{0,1},{3,2},{4,5},{7,6},{8,9},{11,10},{12,13},{15,14},{16,17},{19,... | collective-permute-start | bytes 2359304 | tf_op jit(solution)/shard_map/ppermute | solution.py:182
  104.5 30.9 %collective-permute-start.11 = (bf16[768,512]{1,0:T(8,128)(2,1)}, bf16[768,512]{1,0:T(8,128)(2,1)}, u32[]{:S(2)}, u32[]{:S(2)}) collective-permute-start(bf16[768,512]{1,0:T(8,128)(2,1)} %collective-permute-done.10.rest_0_), channel_id=1, source_target_pairs={{0,4},{1,5},{4,8},{5,9},{6,2},{7,3},{8,12},{9,13},{10,6},{11,7},{1... | collective-permute-start | bytes 2359304 | tf_op jit(solution)/shard_map/ppermute | solution.py:181
  108.9 50.5 %collective-permute-start.19 = (bf16[768,512]{1,0:T(8,128)(2,1)}, bf16[768,512]{1,0:T(8,128)(2,1)}, u32[]{:S(2)}, u32[]{:S(2)}) collective-permute-start(bf16[768,512]{1,0:T(8,128)(2,1)} %collective-permute-done.17.rest_1_), channel_id=1, source_target_pairs={{1,0},{2,3},{5,4},{6,7},{9,8},{10,11},{13,12},{14,15},{17,16},{18,... | collective-permute-start | bytes 2359304 | tf_op jit(solution)/shard_map/ppermute | solution.py:183
  121.4 39.5 %collective-permute-start.5 = (bf16[768,512]{1,0:T(8,128)(2,1)}, bf16[768,512]{1,0:T(8,128)(2,1)}, u32[]{:S(2)}, u32[]{:S(2)}) collective-permute-start(bf16[768,512]{1,0:T(8,128)(2,1)} %collective-permute-done.4.rest_0_), channel_id=1, source_target_pairs={{0,4},{1,5},{4,8},{5,9},{6,2},{7,3},{8,12},{9,13},{10,6},{11,7},{1... | collective-permute-start | bytes 2359304 | tf_op jit(solution)/shard_map/ppermute | solution.py:181
  124.6 60.2 %collective-permute-start.16 = (bf16[768,512]{1,0:T(8,128)(2,1)}, bf16[768,512]{1,0:T(8,128)(2,1)}, u32[]{:S(2)}, u32[]{:S(2)}) collective-permute-start(bf16[768,512]{1,0:T(8,128)(2,1)} %collective-permute-done.14.rest_1_), channel_id=1, source_target_pairs={{1,0},{2,3},{5,4},{6,7},{9,8},{10,11},{13,12},{14,15},{17,16},{18,... | collective-permute-start | bytes 2359304 | tf_op jit(solution)/shard_map/ppermute | solution.py:183
  130.2 65.6 %collective-permute-start.12 = (bf16[768,512]{1,0:T(8,128)(2,1)}, bf16[768,512]{1,0:T(8,128)(2,1)S(1)}, u32[]{:S(2)}, u32[]{:S(2)}) collective-permute-start(bf16[768,512]{1,0:T(8,128)(2,1)} %collective-permute-done.10.rest_0_), channel_id=1, source_target_pairs={{0,1},{3,2},{4,5},{7,6},{8,9},{11,10},{12,13},{15,14},{16,17},{19,... | collective-permute-start | bytes 2359304 | tf_op jit(solution)/shard_map/ppermute | solution.py:182
  135.4 60.4 %collective-permute-start.13 = (bf16[768,512]{1,0:T(8,128)(2,1)}, bf16[768,512]{1,0:T(8,128)(2,1)S(1)}, u32[]{:S(2)}, u32[]{:S(2)}) collective-permute-start(bf16[768,512]{1,0:T(8,128)(2,1)} %collective-permute-done.11.rest_1_), channel_id=1, source_target_pairs={{1,0},{2,3},{5,4},{6,7},{9,8},{10,11},{13,12},{14,15},{17,16},{18,... | collective-permute-start | bytes 2359304 | tf_op jit(solution)/shard_map/ppermute | solution.py:183
  159.4 46.9 %collective-permute-start.6 = (bf16[768,512]{1,0:T(8,128)(2,1)}, bf16[768,512]{1,0:T(8,128)(2,1)S(1)}, u32[]{:S(2)}, u32[]{:S(2)}) collective-permute-start(bf16[768,512]{1,0:T(8,128)(2,1)} %collective-permute-done.4.rest_0_), channel_id=1, source_target_pairs={{0,1},{3,2},{4,5},{7,6},{8,9},{11,10},{12,13},{15,14},{16,17},{19,... | collective-permute-start | bytes 2359304 | tf_op jit(solution)/shard_map/ppermute | solution.py:182
  160.9 45.5 %collective-permute-start.7 = (bf16[768,512]{1,0:T(8,128)(2,1)}, bf16[768,512]{1,0:T(8,128)(2,1)S(1)}, u32[]{:S(2)}, u32[]{:S(2)}) collective-permute-start(bf16[768,512]{1,0:T(8,128)(2,1)} %collective-permute-done.5.rest_1_), channel_id=1, source_target_pairs={{1,0},{2,3},{5,4},{6,7},{9,8},{10,11},{13,12},{14,15},{17,16},{18,... | collective-permute-start | bytes 2359304 | tf_op jit(solution)/shard_map/ppermute | solution.py:183
  (20 other events, 172.9 us)
